TPU v7x, 32 devices: a whole 2x2x4 slice. The times are simulated.
32 devices in a mesh: brow: 8 (over z, core), bcol: 4 (over y, x).
Axes of the slice: x: 2, y: 2, z: 4, core: 2. Of those that a mesh axis runs over, the one named last changes fastest.
Arguments:
- right_side: float32 [16384, 64], P(('brow', 'bcol')), may hold values from -36 to 36
- tiles: bfloat16 [64, 1, 512, 512], P(('brow', 'bcol')), may hold values from -0.03125 to 0.03125
- row_blocks: int32 [64], P(('brow', 'bcol')), may hold values from 0 to 31, as said below
- col_blocks: int32 [64, 1], P(('brow', 'bcol')), may hold values from 0 to 31, as said below
Outputs:
- solution: float32 [16384, 64], P(('brow', 'bcol'))
- residual: float32 [16384, 64], P(('brow', 'bcol'))
Inputs may be any that keep to these rules, and one draw needn't show every extreme that they name: `row_blocks`: the 2 row blocks of one device lie in different groups, the group of block b being b % 4. `col_blocks`: the tile columns of the device at bcol index j are blocks c with c % 4 == j, different within one row slot.
All inputs are finite; a program needn't handle non-finite values.
Results may differ from a plain program's by a relative error of at most 0.0061.
Values may be sent and summed in bfloat16 or wider, within the bound.
A program may use at most 128 MiB of HBM per device.

v0:
```python
import jax
import jax.numpy as jnp
from jax import lax
from jax.sharding import PartitionSpec as P

ITERS = 3
highest = lax.Precision.HIGHEST


def solve_spd(matrix, rhs):
    factor = jnp.linalg.cholesky(matrix)
    return jax.scipy.linalg.cho_solve((factor, True), rhs)


def gram_of(left, right):
    return jnp.dot(left.T, right, precision=highest)


def right_mult(vectors, coeffs):
    return jnp.einsum("...k,kl->...l", vectors, coeffs, precision=highest)


def shards(right_side, tiles, row_blocks, col_blocks):
    groups = lax.axis_size("bcol")
    gblocks = lax.axis_size("brow")
    tile, width = right_side.shape
    slots, per_row = col_blocks.shape
    flat = tile * width
    slot_group = row_blocks % groups
    slot_place = row_blocks // groups
    col_place = col_blocks // groups
    group_ids = jnp.arange(groups, dtype=jnp.int32)
    block_ids = jnp.arange(gblocks, dtype=jnp.int32)
    matches = slot_group[:, None] == group_ids[None, :]
    wanted = jnp.sum(jnp.where(matches, slot_place[:, None], 0), axis=0)
    active = jnp.any(matches, axis=0).astype(jnp.int32)
    asked = lax.all_to_all(
        jnp.stack([wanted, active], axis=1), "bcol", split_axis=0, concat_axis=0, tiled=True
    )
    send_pick = ((asked[:, 0:1] == block_ids[None, :]) & (asked[:, 1:2] == 1)).astype(jnp.float32)
    slot_pick = matches.astype(jnp.float32)
    col_pick = (col_place.reshape(-1)[:, None] == block_ids[None, :]).astype(jnp.float32)
    own_index = lax.axis_index("brow")
    field = lax.all_gather(right_side[None], "brow", axis=0, tiled=True)

    def own(vectors):
        return lax.dynamic_index_in_dim(vectors, own_index, 0, keepdims=False)

    solution = jnp.zeros_like(field)
    residual = field
    direction = field
    rr_now = lax.psum(gram_of(own(residual), own(residual)), ("brow", "bcol"))
    for step in range(ITERS):
        stacked = direction.astype(jnp.bfloat16).reshape(gblocks, flat)
        outgoing = jnp.dot(
            send_pick.astype(jnp.bfloat16), stacked, preferred_element_type=jnp.float32
        ).astype(jnp.bfloat16)
        arrived = lax.all_to_all(outgoing, "bcol", split_axis=0, concat_axis=0, tiled=True)
        row_dir = jnp.dot(
            slot_pick.astype(jnp.bfloat16), arrived, preferred_element_type=jnp.float32
        )
        row_dir = row_dir.astype(jnp.bfloat16).reshape(slots, tile, width)
        col_dir = jnp.dot(
            col_pick.astype(jnp.bfloat16), stacked, preferred_element_type=jnp.float32
        )
        col_dir = col_dir.astype(jnp.bfloat16).reshape(slots, per_row, tile, width)
        turned = jnp.einsum("scab,sak->scbk", tiles, row_dir, preferred_element_type=jnp.float32)
        direct = jnp.einsum("scab,scbk->sak", tiles, col_dir, preferred_element_type=jnp.float32)
        local = jnp.dot(col_pick.T, turned.reshape(slots * per_row, flat), precision=highest)
        pushing = jnp.dot(slot_pick.T, direct.reshape(slots, flat), precision=highest)
        returned = lax.all_to_all(pushing, "bcol", split_axis=0, concat_axis=0, tiled=True)
        local = local + jnp.dot(send_pick.T, returned, precision=highest)
        summed = lax.psum(local.reshape(gblocks, tile, width), "brow")
        image = 3.0 * direction + summed
        curve = lax.psum(gram_of(own(direction), own(image)), ("brow", "bcol"))
        alpha = solve_spd(curve, rr_now)
        solution = solution + right_mult(direction, alpha)
        residual = residual - right_mult(image, alpha)
        if step + 1 < ITERS:
            fresh = lax.psum(gram_of(own(residual), own(residual)), ("brow", "bcol"))
            beta = solve_spd(rr_now, fresh)
            direction = residual + right_mult(direction, beta)
            rr_now = fresh
    return (own(solution), own(residual))


def solution(mesh):
    placed = (
        P(("brow", "bcol"), None),
        P(("brow", "bcol"), None, None, None),
        P(("brow", "bcol")),
        P(("brow", "bcol"), None),
    )
    return jax.shard_map(
        shards,
        mesh=mesh,
        in_specs=placed,
        out_specs=(P(("brow", "bcol"), None), P(("brow", "bcol"), None)),
        check_vma=False,
    )
```

profile of v0, /device:TPU:0, one launch (start us, length us, event | category | flops | bytes accessed | tf_op | source)
XLA Modules:
  0.0 628.7 jit_solution(16731248828745427380)
XLA Ops:
  9.4 5.2 all-to-all-start
  19.4 15.1 %all-gather.3.cloned.1.call-done = f32[4096,64]{0,1:T(8,128)} async-done(((f32[512,64]{0,1:T(8,128)}), f32[4096,64]{0,1:T(8,128)}) %all-gather.3.cloned.1.call-update) | async-done | bytes 1048592 | tf_op jit(solution)/shard_map/all_gather | solution.py:44
  72.3 57.7 %all-reduce.5.cloned.1.call-done = f32[8,512,64]{1,2,0:T(8,128)} async-done(((f32[8,512,64]{1,2,0:T(8,128)}), f32[8,512,64]{1,2,0:T(8,128)}) %all-reduce.5.cloned.1.call-update) | async-done | bytes 1048592 | tf_op jit(solution)/shard_map/psum | solution.py:73
  131.8 40.0 %all-reduce = (f32[64,64]{0,1:T(8,128)S(1)}, f32[64,64]{0,1:T(8,128)S(1)}) all-reduce(f32[64,64]{0,1:T(8,128)S(1)} %fusion.29, f32[64,64]{0,1:T(8,128)S(1)} %fusion.31), channel_id=1, replica_groups=mesh['brow'=8,'bcol'=4] {'brow','bcol'}, use_global_device_ids=true, to_apply=%region_6.8 | all-reduce | flops 8192 | bytes 65536 | tf_op jit(solution)/shard_map/psum | solution.py:52
  171.8 5.8 cholesky.89
  179.0 4.9 custom-call.11
  187.1 40.0 %psum.66 = f32[64,64]{0,1:T(8,128)S(1)} all-reduce(f32[64,64]{0,1:T(8,128)S(1)} %fusion.41), channel_id=1, replica_groups=mesh['brow'=8,'bcol'=4] {'brow','bcol'}, use_global_device_ids=true, to_apply=%region_7.10 | all-reduce | flops 4096 | bytes 32768 | tf_op jit(solution)/shard_map/psum | solution.py:80
  227.1 5.8 cholesky.100
  234.3 4.9 custom-call.12
  255.0 4.7 all-to-all-start.3
  270.7 4.2 all-to-all-start.4
  293.7 5.8 cholesky.122
  300.9 4.9 custom-call.14
  305.8 46.6 %all-reduce.7.cloned.1.call-done = f32[8,512,64]{1,2,0:T(8,128)} async-done(((f32[8,512,64]{1,2,0:T(8,128)}), f32[8,512,64]{1,2,0:T(8,128)}) %all-reduce.7.cloned.1.call-update) | async-done | bytes 1048592 | tf_op jit(solution)/shard_map/psum | solution.py:73
  355.1 39.8 %psum.68 = f32[64,64]{0,1:T(8,128)S(1)} all-reduce(f32[64,64]{0,1:T(8,128)S(1)} %fusion.38), channel_id=1, replica_groups=mesh['brow'=8,'bcol'=4] {'brow','bcol'}, use_global_device_ids=true, to_apply=%region_9.12 | all-reduce | flops 4096 | bytes 32768 | tf_op jit(solution)/shard_map/psum | solution.py:75
  395.0 5.8 cholesky.111
  402.2 4.9 custom-call.13
  412.2 40.0 %psum.69 = f32[64,64]{1,0:T(8,128)S(1)} all-reduce(f32[64,64]{1,0:T(8,128)S(1)} %fusion.36), channel_id=1, replica_groups=mesh['brow'=8,'bcol'=4] {'brow','bcol'}, use_global_device_ids=true, to_apply=%region_10.13 | all-reduce | flops 4096 | bytes 32768 | tf_op jit(solution)/shard_map/psum | solution.py:80
  467.8 4.5 all-to-all-start.5
  482.4 4.2 all-to-all-start.6
  509.6 54.4 %all-reduce.9.cloned.1.call-done = f32[8,512,64]{1,2,0:T(8,128)} async-done(((f32[8,512,64]{1,2,0:T(8,128)}), f32[8,512,64]{1,2,0:T(8,128)}) %all-reduce.9.cloned.1.call-update) | async-done | bytes 1048592 | tf_op jit(solution)/shard_map/psum | solution.py:73
  565.9 39.4 %psum.71 = f32[64,64]{0,1:T(8,128)S(1)} all-reduce(f32[64,64]{0,1:T(8,128)S(1)} %fusion.33), channel_id=1, replica_groups=mesh['brow'=8,'bcol'=4] {'brow','bcol'}, use_global_device_ids=true, to_apply=%region_12.15 | all-reduce | flops 4096 | bytes 32768 | tf_op jit(solution)/shard_map/psum | solution.py:75
  605.4 5.8 cholesky.133
  612.6 4.9 custom-call.15
  (177 shorter events, 164.6 us)
Async XLA Ops:
  7.2 39.7 %copy-start = (bf16[2,1,512,512]{3,2,1,0:T(8,128)(2,1)S(1)}, bf16[2,1,512,512]{3,2,1,0:T(8,128)(2,1)}, u32[]{:S(2)}) copy-start(bf16[2,1,512,512]{3,2,1,0:T(8,128)(2,1)} %param.8) | copy-start | bytes 3145732
  7.2 27.3 %all-gather.3.cloned.1.call-start = ((), (), s32[]{:S(2)}) async-start(), calls=%async_computation.10 | async-start | bytes 1179648 | tf_op jit(solution)/shard_map/all_gather | solution.py:44
  9.4 9.7 %all-to-all-start = ((s32[4,1,2]{2,1,0:T(1,128)}), s32[4,1,2]{2,1,0:T(1,128)S(1)}, u32[]{:S(2)}, u32[]{:S(2)}) async-start(s32[4,1,2]{2,1,0:T(1,128)} %copy.164), calls=%async_computation | async-start | bytes 4096 | tf_op jit(solution)/shard_map/all_to_all | solution.py:37
  43.1 9.4 %all-to-all-start.1 = ((bf16[4,2,16384]{2,1,0:T(2,128)(2,1)}), bf16[4,2,16384]{2,1,0:T(2,128)(2,1)S(1)}, u32[]{:S(2)}, u32[]{:S(2)}) async-start(bf16[4,2,16384]{2,1,0:T(2,128)(2,1)} %reshape.142), calls=%async_computation.1 | async-start | bytes 524288 | tf_op jit(solution)/shard_map/all_to_all | solution.py:58
  52.5 11.6 %all-to-all-start.2 = ((f32[4,1,32768]{2,1,0:T(1,128)}), f32[4,1,32768]{2,1,0:T(1,128)}, u32[]{:S(2)}, u32[]{:S(2)}) async-start(f32[4,1,32768]{2,1,0:T(1,128)} %copy.172), calls=%async_computation.2 | async-start | bytes 1048576 | tf_op jit(solution)/shard_map/all_to_all | solution.py:71
  56.6 73.3 %all-reduce.5.cloned.1.call-start = ((), (), s32[]{:S(2)}) async-start(), calls=%async_computation.7 | async-start | bytes 2097152 | tf_op jit(solution)/shard_map/psum | solution.py:73
  68.6 61.3 %copy-start.1 = (f32[4096,64]{0,1:T(8,128)S(1)}, f32[4096,64]{0,1:T(8,128)}, u32[]{:S(2)}) copy-start(f32[4096,64]{0,1:T(8,128)} %all-gather.3.cloned.1.call-done) | copy-start | bytes 3145732
  129.9 54.6 %copy-start.6 = (f32[8,512,64]{1,2,0:T(8,128)S(1)}, f32[8,512,64]{1,2,0:T(8,128)}, u32[]{:S(2)}) copy-start(f32[8,512,64]{1,2,0:T(8,128)} %all-reduce.5.cloned.1.call-done) | copy-start | bytes 3145732
  184.5 1.3 copy-start.7
  185.8 1.0 copy-start.2
  255.0 15.7 %all-to-all-start.3 = ((bf16[4,2,16384]{2,1,0:T(2,128)(2,1)}), bf16[4,2,16384]{2,1,0:T(2,128)(2,1)S(1)}, u32[]{:S(2)}, u32[]{:S(2)}) async-start(bf16[4,2,16384]{2,1,0:T(2,128)(2,1)} %reshape.144), calls=%async_computation.3 | async-start | bytes 524288 | tf_op jit(solution)/shard_map/all_to_all | solution.py:58
  270.7 13.0 %all-to-all-start.4 = ((f32[4,1,32768]{2,1,0:T(1,128)}), f32[4,1,32768]{2,1,0:T(1,128)}, u32[]{:S(2)}, u32[]{:S(2)}) async-start(f32[4,1,32768]{2,1,0:T(1,128)} %copy.191), calls=%async_computation.4 | async-start | bytes 1048576 | tf_op jit(solution)/shard_map/all_to_all | solution.py:71
  274.9 77.4 %all-reduce.7.cloned.1.call-start = ((), (), s32[]{:S(2)}) async-start(), calls=%async_computation.8 | async-start | bytes 2097152 | tf_op jit(solution)/shard_map/psum | solution.py:73
  353.8 1.0 copy-start.5
  407.6 0.6 copy-start.9
  410.9 1.0 copy-start.4
  452.2 6.4 %copy-start.11 = (f32[64,64]{1,0:T(8,128)}, f32[64,64]{1,0:T(8,128)S(1)}, u32[]{:S(2)}) copy-start(f32[64,64]{1,0:T(8,128)S(1)} %psum.69) | copy-start | bytes 49156
  467.8 14.5 %all-to-all-start.5 = ((bf16[4,2,16384]{2,1,0:T(2,128)(2,1)}), bf16[4,2,16384]{2,1,0:T(2,128)(2,1)S(1)}, u32[]{:S(2)}, u32[]{:S(2)}) async-start(bf16[4,2,16384]{2,1,0:T(2,128)(2,1)} %reshape.146), calls=%async_computation.5 | async-start | bytes 524288 | tf_op jit(solution)/shard_map/all_to_all | solution.py:58
  482.4 13.2 %all-to-all-start.6 = ((f32[4,1,32768]{2,1,0:T(1,128)}), f32[4,1,32768]{2,1,0:T(1,128)}, u32[]{:S(2)}, u32[]{:S(2)}) async-start(f32[4,1,32768]{2,1,0:T(1,128)} %copy.205), calls=%async_computation.6 | async-start | bytes 1048576 | tf_op jit(solution)/shard_map/all_to_all | solution.py:71
  486.6 77.5 %all-reduce.9.cloned.1.call-start = ((), (), s32[]{:S(2)}) async-start(), calls=%async_computation.9 | async-start | bytes 2097152 | tf_op jit(solution)/shard_map/psum | solution.py:73
  502.3 3.2 copy-start.8
  505.4 2.1 copy-start.10
  507.5 56.6 %copy-start.3 = (f32[8,512,64]{1,2,0:T(8,128)S(1)}, f32[8,512,64]{1,2,0:T(8,128)}, u32[]{:S(2)}) copy-start(f32[8,512,64]{1,2,0:T(8,128)} %get-tuple-element.11) | copy-start | bytes 3145732
  509.6 107.9 %copy-start.12 = (f32[64,64]{1,0:T(8,128)S(1)}, f32[64,64]{1,0:T(8,128)}, u32[]{:S(2)}) copy-start(f32[64,64]{1,0:T(8,128)} %copy-done.11) | copy-start | bytes 49156
Sparse Core Ops, SparseCore 0:
  9.6 24.7 all-gather.2
  72.0 57.8 all-reduce.4
  293.8 58.5 all-reduce.6
  505.6 58.4 all-reduce.8
where the time goes:
time: 639 us; the launch traced here: 629 us
  blocking collectives  199 us (31%)
  waiting for transfers between devices  185 us (29%)
  other arithmetic  73 us (11%)
  local copies, waits for them, and re-layouts  67.7 us (11%)
  matrix products  58.6 us (9%)
  starting transfers between devices  30.7 us (5%)
  between operations  14.6 us (2%)
    psum x3, waiting for transfers between devices, shards(): summed = lax.psum(local.reshape(gblocks, tile, width), 'brow')  159 us
    psum x2, blocking collectives, shards(): fresh = lax.psum(gram_of(own(residual), own(residual)), ('brow', 'bcol'))  80 us
    psum x2, blocking collectives, shards(): curve = lax.psum(gram_of(own(direction), own(image)), ('brow', 'bcol'))  79.3 us
    psum x1, blocking collectives, shards(): rr_now = lax.psum(gram_of(own(residual), own(residual)), ('brow', 'bcol'))  40 us
    another operation x15, other arithmetic, solve_spd(): factor = jnp.linalg.cholesky(matrix)  32.6 us
    another operation x10, other arithmetic, solve_spd(): return jax.scipy.linalg.cho_solve((factor, True), rhs)  27.7 us
    reshape x6, local copies, waits for them, and re-layouts, shards(): summed = lax.psum(local.reshape(gblocks, tile, width), 'brow')  18.6 us
    dot_general x8, matrix products, right_mult(): return jnp.einsum('...k,kl->...l', vectors, coeffs, precision=highest)  17 us
  transfers between devices with their start and end apart: 11, of which 7 were waited for; matrix products, arithmetic and copies ran while one was open for 10% of the time, Pallas kernels for 0%

commit v1 on v0

--- a/solution.py
+++ b/solution.py
@@ -2,6 +2,7 @@
 import jax.numpy as jnp
 from jax import lax
 from jax.sharding import PartitionSpec as P
+from jax.lax import psum
 
 ITERS = 3
 highest = lax.Precision.HIGHEST
@@ -49,7 +50,9 @@
     solution = jnp.zeros_like(field)
     residual = field
     direction = field
-    rr_now = lax.psum(gram_of(own(residual), own(residual)), ("brow", "bcol"))
+    slab_in = gram_of(own(residual), own(residual))
+    right_arr = psum(slab_in, "bcol")
+    rr_now = psum(right_arr, "brow")
     for step in range(ITERS):
         stacked = direction.astype(jnp.bfloat16).reshape(gblocks, flat)
         outgoing = jnp.dot(

time: 639 us -> 662 us (1.036)
  blocking collectives: 199 us -> 242 us
  waiting for transfers between devices: 185 us -> 169 us
    psum x2 -> x3, blocking collectives: 79.3 us -> 118 us  [shards(): curve = lax.psum(gram_of(own(direction), own(image)), ('brow', 'bcol'))]
    psum x3, waiting for transfers between devices: 159 us -> 146 us  [shards(): summed = lax.psum(local.reshape(gblocks, tile, width), 'brow')]
    psum x1 -> x2, blocking collectives: 40 us -> 42.7 us  [the longest x1 25.9 us: shards(): rr_now = psum(right_arr, 'brow')]
  transfers between devices with their start and end apart: 11 -> 11, of which waited for: 7 -> 6; matrix products, arithmetic and copies ran while one was open for 10% -> 12% of each run, Pallas kernels for 0% -> 0%
where the time goes in v1:
time: 662 us; the launch traced here: 654 us
  blocking collectives  242 us (37%)
  waiting for transfers between devices  169 us (26%)
  other arithmetic  73 us (11%)
  local copies, waits for them, and re-layouts  67.7 us (10%)
  matrix products  57.2 us (9%)
  starting transfers between devices  30.9 us (5%)
  between operations  14.6 us (2%)
    psum x3, waiting for transfers between devices, shards(): summed = lax.psum(local.reshape(gblocks, tile, width), 'brow')  146 us
    psum x3, blocking collectives, shards(): curve = lax.psum(gram_of(own(direction), own(image)), ('brow', 'bcol'))  118 us
    psum x2, blocking collectives, shards(): fresh = lax.psum(gram_of(own(residual), own(residual)), ('brow', 'bcol'))  80.8 us
    another operation x15, other arithmetic, solve_spd(): factor = jnp.linalg.cholesky(matrix)  32.6 us
    another operation x10, other arithmetic, solve_spd(): return jax.scipy.linalg.cho_solve((factor, True), rhs)  27.7 us
    psum x1, blocking collectives, shards(): rr_now = psum(right_arr, 'brow')  25.9 us
    reshape x6, local copies, waits for them, and re-layouts, shards(): summed = lax.psum(local.reshape(gblocks, tile, width), 'brow')  18.6 us
    dot_general x8, matrix products, right_mult(): return jnp.einsum('...k,kl->...l', vectors, coeffs, precision=highest)  17 us
  transfers between devices with their start and end apart: 11, of which 6 were waited for; matrix products, arithmetic and copies ran while one was open for 12% of the time, Pallas kernels for 0%

profile of v1, /device:TPU:0, one launch (start us, length us, event | category | flops | bytes accessed | tf_op | source)
XLA Modules:
  0.0 654.5 jit_solution(7634322580162986920)
XLA Ops:
  9.4 5.2 all-to-all-start
  19.4 15.1 %all-gather.3.cloned.1.call-done = f32[4096,64]{0,1:T(8,128)} async-done(((f32[512,64]{0,1:T(8,128)}), f32[4096,64]{0,1:T(8,128)}) %all-gather.3.cloned.1.call-update) | async-done | bytes 1048592 | tf_op jit(solution)/shard_map/all_gather | solution.py:45
  47.7 16.8 %psum.72 = f32[64,64]{0,1:T(8,128)S(1)} all-reduce(f32[64,64]{0,1:T(8,128)S(1)} %fusion.29), channel_id=1, replica_groups=mesh['brow'=8,'bcol'=4] {'bcol'}, use_global_device_ids=true, to_apply=%region_6.8 | all-reduce | flops 4096 | bytes 32768 | tf_op jit(solution)/shard_map/psum | solution.py:54
  64.5 25.9 %psum.73 = f32[64,64]{0,1:T(8,128)S(1)} all-reduce(f32[64,64]{0,1:T(8,128)S(1)} %psum.72), channel_id=1, replica_groups=mesh['brow'=8,'bcol'=4] {'brow'}, use_global_device_ids=true, to_apply=%region_7.9 | all-reduce | flops 4096 | bytes 32768 | tf_op jit(solution)/shard_map/psum | solution.py:55
  111.4 5.8 cholesky.100
  118.6 4.9 custom-call.12
  123.5 44.3 %all-reduce.4.cloned.1.call-done = f32[8,512,64]{1,2,0:T(8,128)} async-done(((f32[8,512,64]{1,2,0:T(8,128)}), f32[8,512,64]{1,2,0:T(8,128)}) %all-reduce.4.cloned.1.call-update) | async-done | bytes 1048592 | tf_op jit(solution)/shard_map/psum | solution.py:76
  169.6 39.5 %psum.71 = f32[64,64]{0,1:T(8,128)S(1)} all-reduce(f32[64,64]{0,1:T(8,128)S(1)} %fusion.31), channel_id=1, replica_groups=mesh['brow'=8,'bcol'=4] {'brow','bcol'}, use_global_device_ids=true, to_apply=%region_3.4 | all-reduce | flops 4096 | bytes 32768 | tf_op jit(solution)/shard_map/psum | solution.py:78
  209.2 5.8 cholesky.89
  216.4 4.9 custom-call.11
  224.4 40.3 %psum.74 = f32[64,64]{0,1:T(8,128)S(1)} all-reduce(f32[64,64]{0,1:T(8,128)S(1)} %fusion.41), channel_id=1, replica_groups=mesh['brow'=8,'bcol'=4] {'brow','bcol'}, use_global_device_ids=true, to_apply=%region_8.11 | all-reduce | flops 4096 | bytes 32768 | tf_op jit(solution)/shard_map/psum | solution.py:83
  280.4 4.5 all-to-all-start.3
  319.1 5.8 cholesky.122
  326.3 4.9 custom-call.14
  331.2 46.8 %all-reduce.6.cloned.1.call-done = f32[8,512,64]{1,2,0:T(8,128)} async-done(((f32[8,512,64]{1,2,0:T(8,128)}), f32[8,512,64]{1,2,0:T(8,128)}) %all-reduce.6.cloned.1.call-update) | async-done | bytes 1048592 | tf_op jit(solution)/shard_map/psum | solution.py:76
  380.7 39.5 %psum.76 = f32[64,64]{0,1:T(8,128)S(1)} all-reduce(f32[64,64]{0,1:T(8,128)S(1)} %fusion.38), channel_id=1, replica_groups=mesh['brow'=8,'bcol'=4] {'brow','bcol'}, use_global_device_ids=true, to_apply=%region_10.13 | all-reduce | flops 4096 | bytes 32768 | tf_op jit(solution)/shard_map/psum | solution.py:78
  420.3 5.8 cholesky.111
  427.4 4.9 custom-call.13
  437.4 40.5 %psum.77 = f32[64,64]{1,0:T(8,128)S(1)} all-reduce(f32[64,64]{1,0:T(8,128)S(1)} %fusion.36), channel_id=1, replica_groups=mesh['brow'=8,'bcol'=4] {'brow','bcol'}, use_global_device_ids=true, to_apply=%region_11.14 | all-reduce | flops 4096 | bytes 32768 | tf_op jit(solution)/shard_map/psum | solution.py:83
  493.6 4.5 all-to-all-start.5
  535.4 54.5 %all-reduce.8.cloned.1.call-done = f32[8,512,64]{1,2,0:T(8,128)} async-done(((f32[8,512,64]{1,2,0:T(8,128)}), f32[8,512,64]{1,2,0:T(8,128)}) %all-reduce.8.cloned.1.call-update) | async-done | bytes 1048592 | tf_op jit(solution)/shard_map/psum | solution.py:76
  591.6 39.5 %psum.79 = f32[64,64]{0,1:T(8,128)S(1)} all-reduce(f32[64,64]{0,1:T(8,128)S(1)} %fusion.33), channel_id=1, replica_groups=mesh['brow'=8,'bcol'=4] {'brow','bcol'}, use_global_device_ids=true, to_apply=%region_13.16 | all-reduce | flops 4096 | bytes 32768 | tf_op jit(solution)/shard_map/psum | solution.py:78
  631.2 5.8 cholesky.133
  638.4 4.9 custom-call.15
  (179 shorter events, 169.5 us)
Async XLA Ops:
  7.2 39.9 %copy-start = (bf16[2,1,512,512]{3,2,1,0:T(8,128)(2,1)S(1)}, bf16[2,1,512,512]{3,2,1,0:T(8,128)(2,1)}, u32[]{:S(2)}) copy-start(bf16[2,1,512,512]{3,2,1,0:T(8,128)(2,1)} %param.8) | copy-start | bytes 3145732
  7.2 27.3 %all-gather.3.cloned.1.call-start = ((), (), s32[]{:S(2)}) async-start(), calls=%async_computation.10 | async-start | bytes 1179648 | tf_op jit(solution)/shard_map/all_gather | solution.py:45
  9.4 9.7 %all-to-all-start = ((s32[4,1,2]{2,1,0:T(1,128)}), s32[4,1,2]{2,1,0:T(1,128)S(1)}, u32[]{:S(2)}, u32[]{:S(2)}) async-start(s32[4,1,2]{2,1,0:T(1,128)} %copy.164), calls=%async_computation | async-start | bytes 4096 | tf_op jit(solution)/shard_map/all_to_all | solution.py:38
  43.1 50.1 %all-to-all-start.1 = ((bf16[4,2,16384]{2,1,0:T(2,128)(2,1)}), bf16[4,2,16384]{2,1,0:T(2,128)(2,1)S(1)}, u32[]{:S(2)}, u32[]{:S(2)}) async-start(bf16[4,2,16384]{2,1,0:T(2,128)(2,1)} %reshape.142), calls=%async_computation.1 | async-start | bytes 524288 | tf_op jit(solution)/shard_map/all_to_all | solution.py:61
  93.2 10.8 %all-to-all-start.2 = ((f32[4,1,32768]{2,1,0:T(1,128)}), f32[4,1,32768]{2,1,0:T(1,128)}, u32[]{:S(2)}, u32[]{:S(2)}) async-start(f32[4,1,32768]{2,1,0:T(1,128)} %copy.172), calls=%async_computation.2 | async-start | bytes 1048576 | tf_op jit(solution)/shard_map/all_to_all | solution.py:74
  97.3 70.5 %all-reduce.4.cloned.1.call-start = ((), (), s32[]{:S(2)}) async-start(), calls=%async_computation.7 | async-start | bytes 2097152 | tf_op jit(solution)/shard_map/psum | solution.py:76
  108.2 59.7 %copy-start.1 = (f32[4096,64]{0,1:T(8,128)S(1)}, f32[4096,64]{0,1:T(8,128)}, u32[]{:S(2)}) copy-start(f32[4096,64]{0,1:T(8,128)} %all-gather.3.cloned.1.call-done) | copy-start | bytes 3145732
  167.8 54.0 %copy-start.6 = (f32[8,512,64]{1,2,0:T(8,128)S(1)}, f32[8,512,64]{1,2,0:T(8,128)}, u32[]{:S(2)}) copy-start(f32[8,512,64]{1,2,0:T(8,128)} %all-reduce.4.cloned.1.call-done) | copy-start | bytes 3145732
  221.8 1.3 copy-start.7
  223.1 1.0 copy-start.2
  280.4 15.5 %all-to-all-start.3 = ((bf16[4,2,16384]{2,1,0:T(2,128)(2,1)}), bf16[4,2,16384]{2,1,0:T(2,128)(2,1)S(1)}, u32[]{:S(2)}, u32[]{:S(2)}) async-start(bf16[4,2,16384]{2,1,0:T(2,128)(2,1)} %reshape.144), calls=%async_computation.3 | async-start | bytes 524288 | tf_op jit(solution)/shard_map/all_to_all | solution.py:61
  295.9 13.2 %all-to-all-start.4 = ((f32[4,1,32768]{2,1,0:T(1,128)}), f32[4,1,32768]{2,1,0:T(1,128)}, u32[]{:S(2)}, u32[]{:S(2)}) async-start(f32[4,1,32768]{2,1,0:T(1,128)} %copy.191), calls=%async_computation.4 | async-start | bytes 1048576 | tf_op jit(solution)/shard_map/all_to_all | solution.py:74
  300.1 77.9 %all-reduce.6.cloned.1.call-start = ((), (), s32[]{:S(2)}) async-start(), calls=%async_computation.8 | async-start | bytes 2097152 | tf_op jit(solution)/shard_map/psum | solution.py:76
  379.4 1.0 copy-start.5
  432.8 0.6 copy-start.9
  436.2 1.0 copy-start.4
  477.9 6.4 copy-start.11
  493.6 14.5 %all-to-all-start.5 = ((bf16[4,2,16384]{2,1,0:T(2,128)(2,1)}), bf16[4,2,16384]{2,1,0:T(2,128)(2,1)S(1)}, u32[]{:S(2)}, u32[]{:S(2)}) async-start(bf16[4,2,16384]{2,1,0:T(2,128)(2,1)} %reshape.146), calls=%async_computation.5 | async-start | bytes 524288 | tf_op jit(solution)/shard_map/all_to_all | solution.py:61
  508.1 13.2 %all-to-all-start.6 = ((f32[4,1,32768]{2,1,0:T(1,128)}), f32[4,1,32768]{2,1,0:T(1,128)}, u32[]{:S(2)}, u32[]{:S(2)}) async-start(f32[4,1,32768]{2,1,0:T(1,128)} %copy.205), calls=%async_computation.6 | async-start | bytes 1048576 | tf_op jit(solution)/shard_map/all_to_all | solution.py:74
  512.3 77.6 %all-reduce.8.cloned.1.call-start = ((), (), s32[]{:S(2)}) async-start(), calls=%async_computation.9 | async-start | bytes 2097152 | tf_op jit(solution)/shard_map/psum | solution.py:76
  528.0 3.2 copy-start.8
  531.2 2.1 copy-start.10
  533.3 56.6 %copy-start.3 = (f32[8,512,64]{1,2,0:T(8,128)S(1)}, f32[8,512,64]{1,2,0:T(8,128)}, u32[]{:S(2)}) copy-start(f32[8,512,64]{1,2,0:T(8,128)} %get-tuple-element.9) | copy-start | bytes 3145732
  535.4 107.9 %copy-start.12 = (f32[64,64]{1,0:T(8,128)S(1)}, f32[64,64]{1,0:T(8,128)}, u32[]{:S(2)}) copy-start(f32[64,64]{1,0:T(8,128)} %copy-done.11) | copy-start | bytes 49156
Sparse Core Ops, SparseCore 0:
  9.6 24.7 all-gather.2
  111.6 56.2 all-reduce.3
  319.2 58.6 all-reduce.5
  531.3 58.4 all-reduce.7
